TPU v7x, 128 devices: a whole 4x4x4 slice. The times are simulated.
128 devices in a mesh: dp: 16 (over y, z), expert: 8 (over x, core).
Axes of the slice: x: 4, y: 4, z: 4, core: 2. Of those that a mesh axis runs over, the one named last changes fastest.
Arguments:
- tokens: bfloat16 [16384, 1440], P(('dp', 'expert')), may hold values from -6 to 6
- out_grad: bfloat16 [16384, 1440], P(('dp', 'expert')), may hold values from -6 to 6
- expert_ids: int32 [16384, 4], P(('dp', 'expert')), may hold values from 0 to 7, all different within a row; in each aligned block of 128 rows (0 to 127, 128 to 255, ...) at most 96 rows name the same one
- probs: bfloat16 [16384, 4], P(('dp', 'expert')), may hold values from 0.099609375 to 0.5
- w_gate: bfloat16 [8, 1440, 1440], P('expert'), may hold values from -0.15625 to 0.15625
- w_up: bfloat16 [8, 1440, 1440], P('expert'), may hold values from -0.15625 to 0.15625
- w_down: bfloat16 [8, 1440, 1440], P('expert'), may hold values from -0.15625 to 0.15625
Outputs:
- grad_tokens: bfloat16 [16384, 1440], P(('dp', 'expert'))
- router_grad: bfloat16 [16384, 4], P(('dp', 'expert'))
- grad_gate: float32 [8, 1440, 1440], P('expert', 'dp')
- grad_up: float32 [8, 1440, 1440], P('expert', 'dp')
- grad_down: float32 [8, 1440, 1440], P('expert', 'dp')
Inputs may be any that keep to these rules, and one draw needn't show every extreme that they name: `expert_ids`: each token names 4 different experts; among the tokens of one device no expert is named more than 96 times, a bound that some block reaches.
All inputs are finite; a program needn't handle non-finite values.
Results may differ from a plain program's by a relative error of at most 0.019.
Values may be sent and summed in bfloat16 or wider, within the bound.
A program may use at most 192 MiB of HBM per device.

v0:
```python
import functools

import jax
import jax.numpy as jnp
from jax import lax
from jax.experimental import pallas as pl
from jax.experimental.pallas import tpu as pltpu
from jax.sharding import PartitionSpec as P

BF16, F32 = jnp.bfloat16, jnp.float32
MESH = pl.DeviceIdType.MESH
NT = (((1,), (1,)), ((), ()))
NN = (((1,), (0,)), ((), ()))
CHIP = 256


def mod4(v):
    return lax.rem(v + 8, 4)


def place():
    dp = lax.axis_index("dp")
    ex = lax.axis_index("expert")
    return dp // 4, lax.rem(dp, 4), ex // 2, lax.rem(ex, 2)


def kernel(
    x_h, og_h, ids, probs, wg_h, wu_h, wd_h,
    out, ig_out, routed,
    xg, og, xp, hp, gu, wa, wb, terms, r1, r2, sib, rx, spread, racc,
    load, g_send, g_recv, s_send, s_recv, b_send, b_recv, x_send, x_recv,
):
    y, z, x, c = place()
    dp, ex = y * 4 + z, x * 2 + c

    def at(dp_to=None, ex_to=None):
        return (dp if dp_to is None else dp_to, ex if ex_to is None else ex_to)

    def along(axis, d):
        if axis == "y":
            return at(dp_to=mod4(y + d) * 4 + z)
        if axis == "z":
            return at(dp_to=y * 4 + mod4(z + d))
        return at(ex_to=mod4(x + d) * 2 + c)


    own_x = pltpu.make_async_copy(x_h, xg.at[x, c, 0:1440], load.at[0])
    own_og = pltpu.make_async_copy(og_h, og.at[x, c, 0:1440], load.at[1])
    load_g = pltpu.make_async_copy(wg_h, wa, load.at[2])
    load_u = pltpu.make_async_copy(wu_h, wb, load.at[3])
    load_d = pltpu.make_async_copy(wd_h, wa, load.at[4])
    load_g2 = pltpu.make_async_copy(wg_h, wa, load.at[5])
    for copy in (own_x, own_og, load_g, load_u):
        copy.start()
    sibling = at(ex_to=x * 2 + 1 - c)
    barrier = pltpu.get_barrier_semaphore()
    for to in [along(a, d) for a in "xyz" for d in (1, -1)] + [sibling]:
        pl.semaphore_signal(barrier, inc=1, device_id=to, device_id_type=MESH)

    left, right, far = mod4(x - 1), mod4(x + 1), mod4(x + 2)

    def hop(a, kind, half, got=False):
        buf = (xg, og)[a]
        rows = slice(0, 768) if half == 0 else slice(768, 1456 if a == 0 else 1440)
        n, sent, arrived, to = {
            "right": (0, x, left, along("x", 1)),
            "left": (1, x, right, along("x", -1)),
            "pass_right": (2, left, far, along("x", 1)),
            "pass_left": (3, right, far, along("x", -1)),
            "core_own": (4, x, x, sibling),
            "core_left": (5, left, left, sibling),
            "core_right": (6, right, right, sibling),
            "core_far": (7, far, far, sibling),
        }[kind]
        core = 1 - c if got and n >= 4 else c
        block = buf.at[arrived if got else sent, core, rows]
        return pltpu.make_async_remote_copy(
            src_ref=block, dst_ref=block, send_sem=g_send.at[a, n, half],
            recv_sem=g_recv.at[a, n, half], device_id=to, device_id_type=MESH,
        )

    sent = []

    def send(a, *names):
        for name, half in names:
            hop(a, name, half).start()
            sent.append((a, name, half))

    def got(a, *names):
        for name, half in names:
            hop(a, name, half, got=True).wait_recv()

    def both(name):
        return (name, 0), (name, 1)

    rowid = lax.broadcasted_iota(jnp.int32, (16, 128), 0)
    dense = jnp.zeros((16, 128), F32)
    for k in range(4):
        dense = dense + jnp.where(ids[k : k + 1, :] == rowid, probs[k : k + 1, :].astype(F32), 0.0)
    xg[x, c, 1440:1456, :] = dense.astype(BF16)
    own_x.wait()
    pl.semaphore_wait(barrier, 7)
    send(0, ("right", 0), ("left", 1), *both("core_own"), ("right", 1), ("left", 0))

    row = lax.broadcasted_iota(jnp.int32, (768, 720), 0)
    col = lax.broadcasted_iota(jnp.int32, (768, 720), 1)
    rest = row - 384
    above = lax.div(row, 192) * 360 + lax.div(lax.rem(row, 192), 48) * 90 + lax.rem(row, 48)
    below = lax.rem(lax.div(rest, 48), 2) * 360 + lax.div(rest, 96) * 90 + 48 + lax.rem(rest, 48)
    kept = lax.rem(row, 48) < 42
    picked = ((row < 384) & (above == col)) | ((row >= 384) & kept & (below == col))
    spread[...] = jnp.where(picked, 1.0, 0.0).astype(BF16)

    def flip(w, m):
        for k in range(4):
            n = 384 if k < 3 else 288
            t = w[:, k * 384 : k * 384 + n].T
            for h in range(2):
                r0, r1_ = max(k * 384, h * 720), min(k * 384 + n, h * 720 + 720)
                if r0 < r1_:
                    part = t[r0 - k * 384 : r1_ - k * 384]
                    to = slice(r0 - h * 720, r1_ - h * 720)
                    terms[m, 2 * h, to, :] = part[:, 0:768]
                    terms[m, 2 * h + 1, to, 0:672] = part[:, 768:1440]

    def lanes_of(chip):
        return pl.ds(pl.multiple_of(chip * CHIP, CHIP), CHIP)

    def gate_of(chip):
        parts = []
        for k in range(2):
            rows = xg[chip, k, 1440:1456, :].astype(F32)
            parts.append(jnp.sum(jnp.where(rowid == ex, rows, 0.0), axis=0, keepdims=True))
        return jnp.concatenate(parts, axis=1)

    def place_rows(to, h, v, lanes):
        t = lax.dot_general(spread[...], v, NN, preferred_element_type=F32).astype(BF16)
        to[h * 384 : h * 384 + 384, lanes] = t[0:384]
        for k in range(4):
            r0 = 768 + k * 192 + h * 96
            to[r0 : r0 + 96, lanes] = t[384 + k * 96 : 480 + k * 96]

    def forward(chip):
        lanes = lanes_of(chip)
        gate = gate_of(chip)
        cols = jnp.concatenate([xg[chip, 0, 0:1440, :], xg[chip, 1, 0:1440, :]], axis=1)
        for h in range(2):
            rows = slice(h * 720, h * 720 + 720)
            g, u = [
                lax.dot_general(
                    terms[m, 2 * h, 0:720, :], cols[0:768], NN, preferred_element_type=F32
                )
                + lax.dot_general(
                    terms[m, 2 * h + 1, 0:720, 0:672], cols[768:1440], NN, preferred_element_type=F32
                )
                for m in range(2)
            ]
            s = 0.5 * jnp.tanh(0.5 * g) + 0.5
            gs = g * s
            hidden = gs * u
            gu[0, rows, lanes] = (u * (s + gs * (1.0 - s))).astype(BF16)
            gu[1, rows, lanes] = gs.astype(BF16)
            xp[rows, lanes] = hidden.astype(BF16)
            place_rows(hp, h, (gate * hidden).astype(BF16), lanes)

    def gradient(chip):
        lanes = lanes_of(chip)
        gate = gate_of(chip)
        cols = jnp.concatenate([og[chip, 0, 0:1440, :], og[chip, 1, 0:1440, :]], axis=1)
        total = jnp.zeros((1, CHIP), F32)
        for h in range(2):
            rows = slice(h * 720, h * 720 + 720)
            a = lax.dot_general(wa[rows, :], cols, NN, preferred_element_type=F32)
            pa = gate * a
            gu[0, rows, lanes] = (pa * gu[0, rows, lanes].astype(F32)).astype(BF16)
            gu[1, rows, lanes] = (pa * gu[1, rows, lanes].astype(F32)).astype(BF16)
            hidden = xp[rows, lanes].astype(F32)
            total = total + jnp.sum(hidden * a, axis=0, keepdims=True)
        racc[:, lanes] = total

    def widen(chip):
        for h in range(2):
            rows = slice(h * 720, h * 720 + 720)
            v = jnp.concatenate([xg[chip, 0, rows, :], xg[chip, 1, rows, :]], axis=1)
            place_rows(xp, h, v, lanes_of(chip))

    def way(s):
        first = 1 - s // 2
        d = 1 - 2 * lax.rem(s, 2)
        return first, d

    def step_to(on_y, d):
        return at(dp_to=mod4(y + d * on_y) * 4 + mod4(z + d * (1 - on_y)))

    def chunk(index):
        return pl.ds(pl.multiple_of(index * 192, 64), 192)

    def share(index):
        return pl.ds(pl.multiple_of(index * 48, 16), 48)

    def first_copy(m, s, t):
        on_y, d = way(s)
        pos = y * on_y + z * (1 - on_y)
        src = terms.at[m, s, chunk(mod4(pos - d))] if t == 0 else r1.at[m, s, t - 1]
        return pltpu.make_async_remote_copy(
            src_ref=src, dst_ref=r1.at[m, s, t], send_sem=s_send.at[m, s, t],
            recv_sem=s_recv.at[m, s, t], device_id=step_to(on_y, d), device_id_type=MESH,
        )

    def second_copy(m, s, t):
        on_y, d = way(s)
        pos = z * on_y + y * (1 - on_y)
        src = r1.at[m, s, 2, share(mod4(pos - d))] if t == 0 else r2.at[m, s, t - 1]
        return pltpu.make_async_remote_copy(
            src_ref=src, dst_ref=r2.at[m, s, t], send_sem=s_send.at[m, s, 3 + t],
            recv_sem=s_recv.at[m, s, 3 + t], device_id=step_to(1 - on_y, d), device_id_type=MESH,
        )

    def start(m):
        def body(s, carry):
            r0 = pl.multiple_of((s // 2) * 768, 768)
            c0 = pl.multiple_of(lax.rem(s, 2) * 768, 768)
            a = (hp if m == 0 else xp)[pl.ds(r0, 768), :]
            if m == 0:
                parts = [og[k // 2, k % 2, pl.ds(c0, 768), :] for k in range(8)]
                b = jnp.concatenate(parts, axis=1)
            else:
                b = gu[m - 1, pl.ds(c0, 768), :]
            terms[m, s] = lax.dot_general(a, b, NT, preferred_element_type=F32).astype(BF16)
            first_copy(m, s, 0).start()
            return carry

        lax.fori_loop(0, 4, body, 0)

    def advance(m, stage):
        def body(s, carry):
            on_y, d = way(s)
            if stage < 3:
                pos = y * on_y + z * (1 - on_y)
                first_copy(m, s, stage).wait_recv()
                mine = terms[m, s, chunk(mod4(pos - d * (2 + stage))), :]
                r1[m, s, stage] = r1[m, s, stage] + mine
                if stage < 2:
                    first_copy(m, s, stage + 1).start()
                else:
                    second_copy(m, s, 0).start()
                return carry
            t = stage - 3
            pos = z * on_y + y * (1 - on_y)
            second_copy(m, s, t).wait_recv()
            mine = r1[m, s, 2, share(mod4(pos - d * (2 + t))), :].astype(F32)
            total = r2[m, s, t].astype(F32) + mine
            if t < 2:
                r2[m, s, t] = total.astype(BF16)
                second_copy(m, s, t + 1).start()
            else:
                r0, n = 48 * (s // 2), 48 - 6 * (s // 2)
                lanes = (s % 2) * 768
                width = 768 - 96 * (s % 2)
                out[m, r0 : r0 + n, 0, lanes : lanes + width] = total[0:n, 0:width]
            return carry

        if stage < 5:
            lax.fori_loop(0, 4, body, 0)
        else:
            for s in range(4):
                body(s, 0)

    def ig_chip(chip):
        lanes = slice(chip * CHIP, chip * CHIP + CHIP)

        def body(h, carry):
            rows = pl.ds(pl.multiple_of(h * 720, 16), 720)
            t = lax.dot_general(wa[rows, :], gu[0, 0:1440, lanes], NN, preferred_element_type=F32)
            u = lax.dot_general(wb[rows, :], gu[1, 0:1440, lanes], NN, preferred_element_type=F32)
            t = (t + u).astype(BF16)
            xg[chip, 0, rows, :] = t[:, 0:128]
            xg[chip, 1, rows, :] = t[:, 128:256]
            return carry

        lax.fori_loop(0, 2, body, 0)

    sib_copy = pltpu.make_async_remote_copy(
        src_ref=xg.at[:, 1 - c], dst_ref=sib, send_sem=b_send, recv_sem=b_recv,
        device_id=sibling, device_id_type=MESH,
    )
    halves = ((1, 0, 720), (-1, 720, 736))

    def x_copy(h, t):
        d, lo, n = halves[h]
        src = sib.at[mod4(x - d), lo : lo + n] if t == 0 else rx.at[h, t - 1, 0:n]
        return pltpu.make_async_remote_copy(
            src_ref=src, dst_ref=rx.at[h, t, 0:n], send_sem=x_send.at[h, t],
            recv_sem=x_recv.at[h, t], device_id=along("x", d), device_id_type=MESH,
        )

    def ig_pair():
        sib_copy.wait_recv()
        for k in range(4):
            sib[k] = sib[k] + xg[k, c]
        for h in range(2):
            x_copy(h, 0).start()

    def ig_step(t):
        for h in range(2):
            d, lo, n = halves[h]
            x_copy(h, t).wait_recv()
            own = sib[mod4(x - d * (2 + t)), lo : lo + n]
            if t < 2:
                rx[h, t, 0:n] = rx[h, t, 0:n] + own
                x_copy(h, t + 1).start()
            else:
                total = rx[h, t, 0:n].astype(F32) + own.astype(F32)
                ig_out[lo : lo + 720, :] = total[0:720].astype(BF16)
                if h == 1:
                    for k in range(4):
                        mine = jnp.where(ids[k : k + 1, :] == rowid, total[720:736], 0.0)
                        routed[k : k + 1, :] = jnp.sum(mine, axis=0, keepdims=True).astype(BF16)

    load_g.wait()
    flip(wa, 0)
    load_d.start()
    load_u.wait()
    flip(wb, 1)

    def chip_at(i):
        return mod4(x + i + (i // 2) * (1 - 2 * lax.rem(i, 2)))

    def forwards(i, carry):
        @pl.when(i == 0)
        def _():
            got(0, *both("core_own"))

        @pl.when(i == 1)
        def _():
            got(0, ("right", 0))
            send(0, ("pass_right", 0))
            got(0, ("left", 1))
            send(0, ("pass_left", 1))
            own_og.wait()
            send(1, *both("right"), *both("left"), *both("core_own"))
            got(0, ("left", 0))
            send(0, *both("core_right"))
            got(0, ("right", 1))
            send(0, *both("core_left"))
            got(0, *both("core_right"))

        @pl.when(i == 2)
        def _():
            got(0, *both("core_left"))

        @pl.when(i == 3)
        def _():
            got(0, ("pass_right", 0), ("pass_left", 1))
            send(0, *both("core_far"))
            got(1, ("right", 0))
            send(1, ("pass_right", 0))
            got(1, ("left", 1))
            send(1, ("pass_left", 1))
            got(1, ("left", 0))
            send(1, *both("core_right"))
            got(1, ("right", 1))
            send(1, *both("core_left"))
            got(0, *both("core_far"))

        forward(chip_at(i))
        return carry

    def widens(i, carry):
        widen(chip_at(i))
        return carry

    def gradients(i, carry):
        @pl.when(i == 0)
        def _():
            load_d.wait()
            got(1, *both("core_own"))

        @pl.when(i == 1)
        def _():
            got(1, *both("core_right"))

        @pl.when(i == 2)
        def _():
            got(1, *both("core_left"))

        @pl.when(i == 3)
        def _():
            got(1, ("pass_right", 0), ("pass_left", 1))
            send(1, *both("core_far"))
            lax.fori_loop(0, 3, widens, 0)
            got(1, *both("core_far"))
            start(0)

        gradient(chip_at(i))
        return carry

    lax.fori_loop(0, 4, forwards, 0)
    lax.fori_loop(0, 4, gradients, 0)
    load_g2.start()
    lax.fori_loop(3, 4, widens, 0)
    start(1)
    advance(0, 0)
    start(2)
    for a, name, half in sent:
        if a == 0:
            hop(a, name, half).wait_send()
    for b in range(8):
        part = jnp.broadcast_to(racc[:, b * 128 : (b + 1) * 128], (16, 128))
        xg[b // 2, b % 2, 1440:1456, :] = jnp.where(rowid == ex, part, 0.0).astype(BF16)
    advance(1, 0)
    load_g2.wait()
    ig_chip(0)
    advance(0, 1)
    ig_chip(1)
    advance(2, 0)
    ig_chip(2)
    advance(1, 1)
    ig_chip(3)
    sib_copy.start()
    advance(0, 2)
    advance(2, 1)
    ig_pair()
    advance(0, 3)
    advance(1, 2)
    advance(0, 4)
    ig_step(0)
    advance(1, 3)
    advance(2, 2)
    advance(0, 5)
    advance(1, 4)
    ig_step(1)
    advance(2, 3)
    advance(1, 5)
    ig_step(2)
    advance(2, 4)
    advance(2, 5)
    sib_copy.wait_send()
    for h in range(2):
        for t in range(3):
            x_copy(h, t).wait_send()
    for m in range(3):
        for s in range(4):
            for t in range(3):
                first_copy(m, s, t).wait_send()
                second_copy(m, s, t).wait_send()
    for a, name, half in sent:
        if a == 1:
            hop(a, name, half).wait_send()


def layer(x, og, ids, probs, wg, wu, wd):
    hbm = pl.BlockSpec(memory_space=pl.ANY)
    vmem = pl.BlockSpec(memory_space=pltpu.VMEM)
    return pl.pallas_call(
        kernel,
        out_shape=(
            jax.ShapeDtypeStruct((3, 90, 1, 1440), F32),
            jax.ShapeDtypeStruct((1440, 128), BF16),
            jax.ShapeDtypeStruct((4, 128), BF16),
        ),
        in_specs=[hbm, hbm, vmem, vmem, hbm, hbm, hbm],
        out_specs=(vmem,) * 3,
        scratch_shapes=[
            pltpu.VMEM((4, 2, 1456, 128), BF16),
            pltpu.VMEM((4, 2, 1536, 128), BF16),
            pltpu.VMEM((1536, 1024), BF16),
            pltpu.VMEM((1536, 1024), BF16),
            pltpu.VMEM((2, 1536, 1024), BF16),
            pltpu.VMEM((1440, 1440), BF16),
            pltpu.VMEM((1440, 1440), BF16),
            pltpu.VMEM((3, 4, 768, 768), BF16),
            pltpu.VMEM((3, 4, 3, 192, 768), BF16),
            pltpu.VMEM((3, 4, 3, 48, 768), BF16),
            pltpu.VMEM((4, 1456, 128), BF16),
            pltpu.VMEM((2, 3, 736, 128), BF16),
            pltpu.VMEM((768, 720), BF16),
            pltpu.VMEM((1, 1024), F32),
            pltpu.SemaphoreType.DMA((6,)),
            pltpu.SemaphoreType.DMA((2, 8, 2)),
            pltpu.SemaphoreType.DMA((2, 8, 2)),
            pltpu.SemaphoreType.DMA((3, 4, 6)),
            pltpu.SemaphoreType.DMA((3, 4, 6)),
            pltpu.SemaphoreType.DMA,
            pltpu.SemaphoreType.DMA,
            pltpu.SemaphoreType.DMA((2, 3)),
            pltpu.SemaphoreType.DMA((2, 3)),
        ],
        compiler_params=pltpu.CompilerParams(
            collective_id=0, has_side_effects=True, vmem_limit_bytes=64 * 1024 * 1024
        ),
    )(x, og, ids, probs, wg, wu, wd)


def on_device(tokens, out_grad, expert_ids, probs, w_gate, w_up, w_down):
    out, ig, routed = layer(
        tokens.T, out_grad.T, expert_ids.T, probs.T, w_gate[0], w_up[0], w_down[0]
    )
    down, gate, up = [jnp.transpose(out[m], (1, 0, 2)) for m in range(3)]
    return ig.T, routed.T, gate, up, down


def solution(mesh):
    tok = P(("dp", "expert"), None)
    w = P("expert", None, None)
    g = P("expert", "dp", None)
    return jax.shard_map(
        on_device,
        mesh=mesh,
        in_specs=(tok, tok, tok, tok, w, w, w),
        out_specs=(tok, tok, g, g, g),
        check_vma=False,
    )
```

profile of v0, /device:TPU:0, one launch (start us, length us, event | category | flops | bytes accessed | tf_op | source)
XLA Modules:
  0.0 136.5 jit_solution(1596968578930996360)
XLA Ops:
  0.6 129.7 %shard_map.110 = (f32[3,90,1,1440]{3,2,1,0:T(1,128)}, bf16[1440,128]{1,0:T(8,128)(2,1)}, bf16[4,128]{1,0:T(4,128)(2,1)}) custom-call(bf16[1440,128]{1,0:T(8,128)(2,1)} %bitcast.18, bf16[1440,128]{1,0:T(8,128)(2,1)} %bitcast.19, s32[4,128]{1,0:T(4,128)} %bitcast.21, bf16[4,128]{1,0:T(4,128)(2,1)} %bitcast.22, bf16[1440,1440]{1,0:T(8,128)(2,1)} %bitcast.15, ...), custom_call_target="tpu_custom_call" | custom-call | tf_op jit(solution)/shard_map/pallas_call | solution.py:455
  130.4 3.2 %slice_bitcast_fusion = (f32[1,90,1440]{2,0,1:T(1,128)}, f32[1,90,1440]{2,0,1:T(1,128)}, f32[1,90,1440]{2,0,1:T(1,128)}) fusion(f32[3,90,1,1440]{3,2,1,0:T(1,128)} %get-tuple-element.10), kind=kLoop, calls=%fused_computation | loop fusion | bytes 3110400 | tf_op jit(solution)/shard_map/transpose;squeeze | solution.py:499
  133.6 1.7 %copy.14 = bf16[128,1440]{0,1:T(8,128)(2,1)} copy(bf16[128,1440]{0,1:T(8,128)(2,1)} %bitcast.20) | data formatting | bytes 737280
  135.3 1.2 copy.15
where the time goes:
time: 137 us
  Pallas kernels  130 us (95%)
  local copies, waits for them, and re-layouts  6.17 us (5%)
    pallas_call x1, Pallas kernels, layer(): pl.pallas_call(kernel, out_shape=(jax.ShapeDtypeStruct((3, 90, 1, 1440),...  130 us
    another operation x1, local copies, waits for them, and re-layouts, on_device(): down, gate, up = [jnp.transpose(out[m], (1, 0, 2)) for m in range(3)]  3.18 us
    unnamed x2, local copies, waits for them, and re-layouts  2.98 us

commit v1 on v0

--- a/solution.py
+++ b/solution.py
@@ -100,7 +100,7 @@
     xg[x, c, 1440:1456, :] = dense.astype(BF16)
     own_x.wait()
     pl.semaphore_wait(barrier, 7)
-    send(0, ("right", 0), ("left", 1), *both("core_own"), ("right", 1), ("left", 0))
+    send(0, ("right", 0), ("left", 1), *both("core_own"))
 
     row = lax.broadcasted_iota(jnp.int32, (768, 720), 0)
     col = lax.broadcasted_iota(jnp.int32, (768, 720), 1)
@@ -201,19 +201,21 @@
     def first_copy(m, s, t):
         on_y, d = way(s)
         pos = y * on_y + z * (1 - on_y)
-        src = terms.at[m, s, chunk(mod4(pos - d))] if t == 0 else r1.at[m, s, t - 1]
+        go = -d if t == 1 else d
+        src = r1.at[m, s, 0] if t == 2 else terms.at[m, s, chunk(mod4(pos + (2 * d, -d)[t]))]
         return pltpu.make_async_remote_copy(
             src_ref=src, dst_ref=r1.at[m, s, t], send_sem=s_send.at[m, s, t],
-            recv_sem=s_recv.at[m, s, t], device_id=step_to(on_y, d), device_id_type=MESH,
+            recv_sem=s_recv.at[m, s, t], device_id=step_to(on_y, go), device_id_type=MESH,
         )
 
     def second_copy(m, s, t):
         on_y, d = way(s)
         pos = z * on_y + y * (1 - on_y)
-        src = r1.at[m, s, 2, share(mod4(pos - d))] if t == 0 else r2.at[m, s, t - 1]
+        go = -d if t == 1 else d
+        src = r2.at[m, s, 0] if t == 2 else r1.at[m, s, 2, share(mod4(pos + (2 * d, -d)[t]))]
         return pltpu.make_async_remote_copy(
             src_ref=src, dst_ref=r2.at[m, s, t], send_sem=s_send.at[m, s, 3 + t],
-            recv_sem=s_recv.at[m, s, 3 + t], device_id=step_to(1 - on_y, d), device_id_type=MESH,
+            recv_sem=s_recv.at[m, s, 3 + t], device_id=step_to(1 - on_y, go), device_id_type=MESH,
         )
 
     def start(m):
@@ -228,6 +230,7 @@
                 b = gu[m - 1, pl.ds(c0, 768), :]
             terms[m, s] = lax.dot_general(a, b, NT, preferred_element_type=F32).astype(BF16)
             first_copy(m, s, 0).start()
+            first_copy(m, s, 1).start()
             return carry
 
         lax.fori_loop(0, 4, body, 0)
@@ -235,32 +238,37 @@
     def advance(m, stage):
         def body(s, carry):
             on_y, d = way(s)
-            if stage < 3:
+            if stage < 2:
                 pos = y * on_y + z * (1 - on_y)
-                first_copy(m, s, stage).wait_recv()
-                mine = terms[m, s, chunk(mod4(pos - d * (2 + stage))), :]
-                r1[m, s, stage] = r1[m, s, stage] + mine
-                if stage < 2:
-                    first_copy(m, s, stage + 1).start()
+                if stage == 0:
+                    first_copy(m, s, 0).wait_recv()
+                    r1[m, s, 0] = r1[m, s, 0] + terms[m, s, chunk(mod4(pos + d)), :]
+                    first_copy(m, s, 2).start()
                 else:
+                    first_copy(m, s, 1).wait_recv()
+                    first_copy(m, s, 2).wait_recv()
+                    mine = terms[m, s, chunk(pos), :].astype(F32) + r1[m, s, 1].astype(F32)
+                    r1[m, s, 2] = (r1[m, s, 2].astype(F32) + mine).astype(BF16)
                     second_copy(m, s, 0).start()
+                    second_copy(m, s, 1).start()
                 return carry
-            t = stage - 3
             pos = z * on_y + y * (1 - on_y)
-            second_copy(m, s, t).wait_recv()
-            mine = r1[m, s, 2, share(mod4(pos - d * (2 + t))), :].astype(F32)
-            total = r2[m, s, t].astype(F32) + mine
-            if t < 2:
-                r2[m, s, t] = total.astype(BF16)
-                second_copy(m, s, t + 1).start()
+            if stage == 2:
+                second_copy(m, s, 0).wait_recv()
+                r2[m, s, 0] = r2[m, s, 0] + r1[m, s, 2, share(mod4(pos + d)), :]
+                second_copy(m, s, 2).start()
             else:
+                second_copy(m, s, 1).wait_recv()
+                second_copy(m, s, 2).wait_recv()
+                mine = r1[m, s, 2, share(pos), :].astype(F32)
+                total = r2[m, s, 1].astype(F32) + r2[m, s, 2].astype(F32) + mine
                 r0, n = 48 * (s // 2), 48 - 6 * (s // 2)
                 lanes = (s % 2) * 768
                 width = 768 - 96 * (s % 2)
                 out[m, r0 : r0 + n, 0, lanes : lanes + width] = total[0:n, 0:width]
             return carry
 
-        if stage < 5:
+        if stage < 3:
             lax.fori_loop(0, 4, body, 0)
         else:
             for s in range(4):
@@ -322,6 +330,12 @@
     load_d.start()
     load_u.wait()
     flip(wb, 1)
+    hop(0, "right", 0).wait_send()
+    sent.remove((0, "right", 0))
+    send(0, ("right", 1))
+    hop(0, "left", 1).wait_send()
+    sent.remove((0, "left", 1))
+    send(0, ("left", 0))
 
     def chip_at(i):
         return mod4(x + i + (i // 2) * (1 - 2 * lax.rem(i, 2)))
@@ -353,6 +367,23 @@
         def _():
             got(0, ("pass_right", 0), ("pass_left", 1))
             send(0, *both("core_far"))
+            got(0, *both("core_far"))
+
+        forward(chip_at(i))
+        return carry
+
+    def widens(i, carry):
+        widen(chip_at(i))
+        return carry
+
+    def gradients(i, carry):
+        @pl.when(i == 0)
+        def _():
+            load_d.wait()
+            got(1, *both("core_own"))
+
+        @pl.when(i == 1)
+        def _():
             got(1, ("right", 0))
             send(1, ("pass_right", 0))
             got(1, ("left", 1))
@@ -361,23 +392,6 @@
             send(1, *both("core_right"))
             got(1, ("right", 1))
             send(1, *both("core_left"))
-            got(0, *both("core_far"))
-
-        forward(chip_at(i))
-        return carry
-
-    def widens(i, carry):
-        widen(chip_at(i))
-        return carry
-
-    def gradients(i, carry):
-        @pl.when(i == 0)
-        def _():
-            load_d.wait()
-            got(1, *both("core_own"))
-
-        @pl.when(i == 1)
-        def _():
             got(1, *both("core_right"))
 
         @pl.when(i == 2)
@@ -400,7 +414,6 @@
     load_g2.start()
     lax.fori_loop(3, 4, widens, 0)
     start(1)
-    advance(0, 0)
     start(2)
     for a, name, half in sent:
         if a == 0:
@@ -408,33 +421,28 @@
     for b in range(8):
         part = jnp.broadcast_to(racc[:, b * 128 : (b + 1) * 128], (16, 128))
         xg[b // 2, b % 2, 1440:1456, :] = jnp.where(rowid == ex, part, 0.0).astype(BF16)
-    advance(1, 0)
     load_g2.wait()
     ig_chip(0)
-    advance(0, 1)
     ig_chip(1)
-    advance(2, 0)
+    advance(0, 0)
     ig_chip(2)
-    advance(1, 1)
     ig_chip(3)
     sib_copy.start()
+    advance(1, 0)
+    advance(2, 0)
+    ig_pair()
+    advance(0, 1)
+    ig_step(0)
     advance(0, 2)
+    advance(1, 1)
     advance(2, 1)
-    ig_pair()
+    ig_step(1)
     advance(0, 3)
     advance(1, 2)
-    advance(0, 4)
-    ig_step(0)
+    advance(2, 2)
+    ig_step(2)
     advance(1, 3)
-    advance(2, 2)
-    advance(0, 5)
-    advance(1, 4)
-    ig_step(1)
     advance(2, 3)
-    advance(1, 5)
-    ig_step(2)
-    advance(2, 4)
-    advance(2, 5)
     sib_copy.wait_send()
     for h in range(2):
         for t in range(3):

time: 137 us -> 131 us (0.956)
  Pallas kernels: 130 us -> 124 us
    pallas_call x1, Pallas kernels: 130 us -> 124 us  [layer(): pl.pallas_call(kernel, out_shape=(jax.ShapeDtypeStruct((3, 90, 1, 1440),...]
where the time goes in v1:
time: 131 us
  Pallas kernels  124 us (95%)
  local copies, waits for them, and re-layouts  6.17 us (5%)
    pallas_call x1, Pallas kernels, layer(): pl.pallas_call(kernel, out_shape=(jax.ShapeDtypeStruct((3, 90, 1, 1440),...  124 us
    another operation x1, local copies, waits for them, and re-layouts, on_device(): down, gate, up = [jnp.transpose(out[m], (1, 0, 2)) for m in range(3)]  3.18 us
    unnamed x2, local copies, waits for them, and re-layouts  2.98 us

profile of v1, /device:TPU:0, one launch (start us, length us, event | category | flops | bytes accessed | tf_op | source)
XLA Modules:
  0.0 130.6 jit_solution(13949301580017202609)
XLA Ops:
  0.6 123.7 %shard_map.110 = (f32[3,90,1,1440]{3,2,1,0:T(1,128)}, bf16[1440,128]{1,0:T(8,128)(2,1)}, bf16[4,128]{1,0:T(4,128)(2,1)}) custom-call(bf16[1440,128]{1,0:T(8,128)(2,1)} %bitcast.18, bf16[1440,128]{1,0:T(8,128)(2,1)} %bitcast.19, s32[4,128]{1,0:T(4,128)} %bitcast.21, bf16[4,128]{1,0:T(4,128)(2,1)} %bitcast.22, bf16[1440,1440]{1,0:T(8,128)(2,1)} %bitcast.15, ...), custom_call_target="tpu_custom_call" | custom-call | tf_op jit(solution)/shard_map/pallas_call | solution.py:463
  124.4 3.2 %slice_bitcast_fusion = (f32[1,90,1440]{2,0,1:T(1,128)}, f32[1,90,1440]{2,0,1:T(1,128)}, f32[1,90,1440]{2,0,1:T(1,128)}) fusion(f32[3,90,1,1440]{3,2,1,0:T(1,128)} %get-tuple-element.10), kind=kLoop, calls=%fused_computation | loop fusion | bytes 3110400 | tf_op jit(solution)/shard_map/transpose;squeeze | solution.py:507
  127.6 1.7 %copy.14 = bf16[128,1440]{0,1:T(8,128)(2,1)} copy(bf16[128,1440]{0,1:T(8,128)(2,1)} %bitcast.20) | data formatting | bytes 737280
  129.3 1.2 copy.15

commit v2 on v1

--- a/solution.py
+++ b/solution.py
@@ -50,8 +50,7 @@
     load_u = pltpu.make_async_copy(wu_h, wb, load.at[3])
     load_d = pltpu.make_async_copy(wd_h, wa, load.at[4])
     load_g2 = pltpu.make_async_copy(wg_h, wa, load.at[5])
-    for copy in (own_x, own_og, load_g, load_u):
-        copy.start()
+    own_x.start()
     sibling = at(ex_to=x * 2 + 1 - c)
     barrier = pltpu.get_barrier_semaphore()
     for to in [along(a, d) for a in "xyz" for d in (1, -1)] + [sibling]:
@@ -99,17 +98,18 @@
         dense = dense + jnp.where(ids[k : k + 1, :] == rowid, probs[k : k + 1, :].astype(F32), 0.0)
     xg[x, c, 1440:1456, :] = dense.astype(BF16)
     own_x.wait()
-    pl.semaphore_wait(barrier, 7)
-    send(0, ("right", 0), ("left", 1), *both("core_own"))
-
-    row = lax.broadcasted_iota(jnp.int32, (768, 720), 0)
-    col = lax.broadcasted_iota(jnp.int32, (768, 720), 1)
+    for copy in (load_g, load_u, own_og):
+        copy.start()
+    row = lax.broadcasted_iota(jnp.int32, (768, 1), 0)
     rest = row - 384
     above = lax.div(row, 192) * 360 + lax.div(lax.rem(row, 192), 48) * 90 + lax.rem(row, 48)
     below = lax.rem(lax.div(rest, 48), 2) * 360 + lax.div(rest, 96) * 90 + 48 + lax.rem(rest, 48)
-    kept = lax.rem(row, 48) < 42
-    picked = ((row < 384) & (above == col)) | ((row >= 384) & kept & (below == col))
+    below = jnp.where(lax.rem(row, 48) < 42, below, -1)
+    source = jnp.where(row < 384, above, below)
+    picked = source == lax.broadcasted_iota(jnp.int32, (768, 720), 1)
     spread[...] = jnp.where(picked, 1.0, 0.0).astype(BF16)
+    pl.semaphore_wait(barrier, 7)
+    send(0, ("right", 0), ("left", 1), *both("core_own"))
 
     def flip(w, m):
         for k in range(4):
@@ -352,7 +352,7 @@
             got(0, ("left", 1))
             send(0, ("pass_left", 1))
             own_og.wait()
-            send(1, *both("right"), *both("left"), *both("core_own"))
+            send(1, ("right", 0), ("left", 1), *both("core_own"))
             got(0, ("left", 0))
             send(0, *both("core_right"))
             got(0, ("right", 1))
@@ -361,33 +361,34 @@
 
         @pl.when(i == 2)
         def _():
+            send(1, ("right", 1), ("left", 0))
             got(0, *both("core_left"))
 
         @pl.when(i == 3)
         def _():
             got(0, ("pass_right", 0), ("pass_left", 1))
             send(0, *both("core_far"))
-            got(0, *both("core_far"))
-
-        forward(chip_at(i))
-        return carry
-
-    def widens(i, carry):
-        widen(chip_at(i))
-        return carry
-
-    def gradients(i, carry):
-        @pl.when(i == 0)
-        def _():
-            load_d.wait()
-            got(1, *both("core_own"))
-
-        @pl.when(i == 1)
-        def _():
             got(1, ("right", 0))
             send(1, ("pass_right", 0))
             got(1, ("left", 1))
             send(1, ("pass_left", 1))
+            got(0, *both("core_far"))
+
+        forward(chip_at(i))
+        return carry
+
+    def widens(i, carry):
+        widen(chip_at(i))
+        return carry
+
+    def gradients(i, carry):
+        @pl.when(i == 0)
+        def _():
+            load_d.wait()
+            got(1, *both("core_own"))
+
+        @pl.when(i == 1)
+        def _():
             got(1, ("left", 0))
             send(1, *both("core_right"))
             got(1, ("right", 1))
@@ -402,7 +403,6 @@
         def _():
             got(1, ("pass_right", 0), ("pass_left", 1))
             send(1, *both("core_far"))
-            lax.fori_loop(0, 3, widens, 0)
             got(1, *both("core_far"))
             start(0)
 
@@ -412,7 +412,7 @@
     lax.fori_loop(0, 4, forwards, 0)
     lax.fori_loop(0, 4, gradients, 0)
     load_g2.start()
-    lax.fori_loop(3, 4, widens, 0)
+    lax.fori_loop(0, 4, widens, 0)
     start(1)
     start(2)
     for a, name, half in sent:

time: 131 us -> 130 us (level)
  no operation moved by 1% of the time
where the time goes in v2:
time: 130 us
  Pallas kernels  123 us (95%)
  local copies, waits for them, and re-layouts  6.17 us (5%)
    pallas_call x1, Pallas kernels, layer(): pl.pallas_call(kernel, out_shape=(jax.ShapeDtypeStruct((3, 90, 1, 1440),...  123 us
    another operation x1, local copies, waits for them, and re-layouts, on_device(): down, gate, up = [jnp.transpose(out[m], (1, 0, 2)) for m in range(3)]  3.18 us
    unnamed x2, local copies, waits for them, and re-layouts  2.98 us

profile of v2, /device:TPU:0, one launch (start us, length us, event | category | flops | bytes accessed | tf_op | source)
XLA Modules:
  0.0 129.5 jit_solution(17676129651996963934)
XLA Ops:
  0.6 122.7 %shard_map.110 = (f32[3,90,1,1440]{3,2,1,0:T(1,128)}, bf16[1440,128]{1,0:T(8,128)(2,1)}, bf16[4,128]{1,0:T(4,128)(2,1)}) custom-call(bf16[1440,128]{1,0:T(8,128)(2,1)} %bitcast.18, bf16[1440,128]{1,0:T(8,128)(2,1)} %bitcast.19, s32[4,128]{1,0:T(4,128)} %bitcast.21, bf16[4,128]{1,0:T(4,128)(2,1)} %bitcast.22, bf16[1440,1440]{1,0:T(8,128)(2,1)} %bitcast.15, ...), custom_call_target="tpu_custom_call" | custom-call | tf_op jit(solution)/shard_map/pallas_call | solution.py:463
  123.3 3.2 %slice_bitcast_fusion = (f32[1,90,1440]{2,0,1:T(1,128)}, f32[1,90,1440]{2,0,1:T(1,128)}, f32[1,90,1440]{2,0,1:T(1,128)}) fusion(f32[3,90,1,1440]{3,2,1,0:T(1,128)} %get-tuple-element.10), kind=kLoop, calls=%fused_computation | loop fusion | bytes 3110400 | tf_op jit(solution)/shard_map/transpose;squeeze | solution.py:507
  126.5 1.7 %copy.14 = bf16[128,1440]{0,1:T(8,128)(2,1)} copy(bf16[128,1440]{0,1:T(8,128)(2,1)} %bitcast.20) | data formatting | bytes 737280
  128.3 1.2 copy.15

commit v3 on v2

--- a/solution.py
+++ b/solution.py
@@ -26,9 +26,9 @@
 
 def kernel(
     x_h, og_h, ids, probs, wg_h, wu_h, wd_h,
-    out, ig_out, routed,
-    xg, og, xp, hp, gu, wa, wb, terms, r1, r2, sib, rx, spread, racc,
-    load, g_send, g_recv, s_send, s_recv, b_send, b_recv, x_send, x_recv,
+    out_h, ig_out, routed,
+    xg, og, xp, hp, gu, wa, wb, terms, r1, r2, sib, rx, spread, racc, out,
+    load, g_send, g_recv, s_send, s_recv, b_send, b_recv, x_send, x_recv, store,
 ):
     y, z, x, c = place()
     dp, ex = y * 4 + z, x * 2 + c
@@ -230,10 +230,17 @@
                 b = gu[m - 1, pl.ds(c0, 768), :]
             terms[m, s] = lax.dot_general(a, b, NT, preferred_element_type=F32).astype(BF16)
             first_copy(m, s, 0).start()
+            return carry
+
+        def near(s, carry):
             first_copy(m, s, 1).start()
             return carry
 
         lax.fori_loop(0, 4, body, 0)
+        lax.fori_loop(0, 4, near, 0)
+
+    def stored(m):
+        return pltpu.make_async_copy(out.at[m], out_h.at[m], store.at[m])
 
     def advance(m, stage):
         def body(s, carry):
@@ -273,6 +280,7 @@
         else:
             for s in range(4):
                 body(s, 0)
+            stored(m).start()
 
     def ig_chip(chip):
         lanes = slice(chip * CHIP, chip * CHIP + CHIP)
@@ -443,6 +451,8 @@
     ig_step(2)
     advance(1, 3)
     advance(2, 3)
+    for m in range(3):
+        stored(m).wait()
     sib_copy.wait_send()
     for h in range(2):
         for t in range(3):
@@ -468,7 +478,7 @@
             jax.ShapeDtypeStruct((4, 128), BF16),
         ),
         in_specs=[hbm, hbm, vmem, vmem, hbm, hbm, hbm],
-        out_specs=(vmem,) * 3,
+        out_specs=(hbm, vmem, vmem),
         scratch_shapes=[
             pltpu.VMEM((4, 2, 1456, 128), BF16),
             pltpu.VMEM((4, 2, 1536, 128), BF16),
@@ -484,6 +494,7 @@
             pltpu.VMEM((2, 3, 736, 128), BF16),
             pltpu.VMEM((768, 720), BF16),
             pltpu.VMEM((1, 1024), F32),
+            pltpu.VMEM((3, 90, 1, 1440), F32),
             pltpu.SemaphoreType.DMA((6,)),
             pltpu.SemaphoreType.DMA((2, 8, 2)),
             pltpu.SemaphoreType.DMA((2, 8, 2)),
@@ -493,6 +504,7 @@
             pltpu.SemaphoreType.DMA,
             pltpu.SemaphoreType.DMA((2, 3)),
             pltpu.SemaphoreType.DMA((2, 3)),
+            pltpu.SemaphoreType.DMA((3,)),
         ],
         compiler_params=pltpu.CompilerParams(
             collective_id=0, has_side_effects=True, vmem_limit_bytes=64 * 1024 * 1024

time: 130 us -> 131 us (level)
    pallas_call x1, Pallas kernels: 123 us -> 124 us  [layer(): pl.pallas_call(kernel, out_shape=(jax.ShapeDtypeStruct((3, 90, 1, 1440),...]
where the time goes in v3:
time: 131 us
  Pallas kernels  124 us (95%)
  local copies, waits for them, and re-layouts  6.17 us (5%)
    pallas_call x1, Pallas kernels, layer(): pl.pallas_call(kernel, out_shape=(jax.ShapeDtypeStruct((3, 90, 1, 1440),...  124 us
    another operation x1, local copies, waits for them, and re-layouts, on_device(): down, gate, up = [jnp.transpose(out[m], (1, 0, 2)) for m in range(3)]  3.18 us
    unnamed x2, local copies, waits for them, and re-layouts  2.98 us

profile of v3, /device:TPU:0, one launch (start us, length us, event | category | flops | bytes accessed | tf_op | source)
XLA Modules:
  0.0 131.1 jit_solution(2438421320942439207)
XLA Ops:
  0.6 124.3 %shard_map.110 = (f32[3,90,1,1440]{3,2,1,0:T(1,128)}, bf16[1440,128]{1,0:T(8,128)(2,1)}, bf16[4,128]{1,0:T(4,128)(2,1)}) custom-call(bf16[1440,128]{1,0:T(8,128)(2,1)} %bitcast.18, bf16[1440,128]{1,0:T(8,128)(2,1)} %bitcast.19, s32[4,128]{1,0:T(4,128)} %bitcast.21, bf16[4,128]{1,0:T(4,128)(2,1)} %bitcast.22, bf16[1440,1440]{1,0:T(8,128)(2,1)} %bitcast.15, ...), custom_call_target="tpu_custom_call" | custom-call | tf_op jit(solution)/shard_map/pallas_call | solution.py:473
  125.0 3.2 %slice_bitcast_fusion = (f32[1,90,1440]{2,0,1:T(1,128)}, f32[1,90,1440]{2,0,1:T(1,128)}, f32[1,90,1440]{2,0,1:T(1,128)}) fusion(f32[3,90,1,1440]{3,2,1,0:T(1,128)} %get-tuple-element.10), kind=kLoop, calls=%fused_computation | loop fusion | bytes 3110400 | tf_op jit(solution)/shard_map/transpose;squeeze | solution.py:519
  128.2 1.7 %copy.14 = bf16[128,1440]{0,1:T(8,128)(2,1)} copy(bf16[128,1440]{0,1:T(8,128)(2,1)} %bitcast.20) | data formatting | bytes 737280
  129.9 1.2 copy.15
